TPU v7x, 32 devices: a whole 2x2x4 slice. The times are simulated.
32 devices in a mesh: seq: 8 (over y, x, core), head: 4 (over z).
Axes of the slice: x: 2, y: 2, z: 4, core: 2. Of those that a mesh axis runs over, the one named last changes fastest.
Arguments:
- queries: bfloat16 [1, 2048, 4096], P(None, 'seq', 'head'), may hold values from -6 to 6
- keys: bfloat16 [1, 2048, 4096], P(None, 'seq', 'head'), may hold values from -6 to 6
- values: bfloat16 [1, 2048, 4096], P(None, 'seq', 'head'), may hold values from -6 to 6
- out_weight: bfloat16 [4096, 4096], P('head'), may hold values from -0.09375 to 0.09375
- out_grad: bfloat16 [1, 2048, 4096], P(None, 'seq', 'head'), may hold values from -6 to 6
- block_doc: int32 [1, 8], replicated, may hold values from 0 to 2, never falling along the last dimension, each value on 1 to 6 neighbouring positions
Outputs:
- context: bfloat16 [1, 2048, 4096], P(None, 'seq', 'head')
- query_grad: bfloat16 [1, 2048, 4096], P(None, 'seq', 'head')
- key_grad: bfloat16 [1, 2048, 4096], P(None, 'seq', 'head')
- value_grad: bfloat16 [1, 2048, 4096], P(None, 'seq', 'head')
- weight_grad: bfloat16 [4096, 4096], P('head', 'seq')
Inputs may be any that keep to these rules, and one draw needn't show every extreme that they name: `block_doc`: document numbers never fall along a pack, every document holds whole leaf blocks, and one document covers exactly 6 blocks.
All inputs are finite; a program needn't handle non-finite values.
Results may differ from a plain program's by a relative error of at most 0.019.
Values may be sent and summed in bfloat16 or wider, within the bound.
A program may use at most 128 MiB of HBM per device.

v0:
```python
import functools
import math

import jax
import jax.numpy as jnp
from jax import lax
from jax.experimental import pallas as pl
from jax.experimental.pallas import tpu as pltpu
from jax.sharding import PartitionSpec as P

DH = 128
GROUP_HEADS = 2
F32 = jnp.float32
BF16 = jnp.bfloat16


def flipped(index, mask):
    out = index
    bit = 1
    while bit <= mask:
        if mask & bit:
            out = out + (1 - 2 * lax.rem(lax.div(index, jnp.int32(bit)), jnp.int32(2))) * bit
        bit *= 2
    return out


def dot_nn(a, b):
    return lax.dot_general(a, b, (((1,), (0,)), ((), ())), preferred_element_type=F32)


def dot_nt(a, b):
    return lax.dot_general(a, b, (((1,), (1,)), ((), ())), preferred_element_type=F32)


def dot_tn(a, b):
    return lax.dot_general(a, b, (((0,), (0,)), ((), ())), preferred_element_type=F32)


def pieces_of(seq_count, leaf):
    rows, starts, at = {}, {}, 0
    for parity in (0, 1):
        for o in range(parity, seq_count, 2):
            level = max(o.bit_length() - 1, 0)
            rows[o], starts[o] = leaf >> level, at
            at += rows[o]
    return rows, starts, at


def kernel(seq_count, head_count, leaf, feats,
           doc, q_ref, k_ref, v_ref, og_ref, w_ref,
           ctx_out, dq_out, dk_out, dv_out, wg_out,
           wv, ogf, kc, pb, probs, ctxs, ogs, cga, cgt, own, dbuf, pair, back, acc,
           s_w, s_up, s_dn, r_z, s_kv, r_kv, s_a, r_a, s_c, r_c, s_p, r_p, s_g, r_g):
    me = lax.axis_index("seq")
    z = lax.axis_index("head")
    partner = flipped(me, 1)
    levels = seq_count.bit_length() - 1
    rows, starts, cols = pieces_of(seq_count, leaf)
    half = cols // 2
    heads = feats // DH
    gcols = GROUP_HEADS * DH
    groups = feats // gcols
    per_shard = seq_count // head_count
    kcols = feats // per_shard
    scaling = 1.0 / math.sqrt(DH)

    def remote(src, dst, send, recv, **where):
        return pltpu.make_async_remote_copy(
            src_ref=src, dst_ref=dst, send_sem=send, recv_sem=recv,
            device_id=where, device_id_type=pl.DeviceIdType.MESH)

    def arrived(dst, recv):
        remote(dst, dst, recv, recv, seq=partner).wait_recv()

    def w_copy(zp):
        return pltpu.make_async_copy(
            w_ref.at[:, pl.ds(zp * feats, feats)], wv.at[zp], s_w.at[zp])

    def up_copy(zp):
        return remote(ogf.at[zp], ogf.at[zp], s_up.at[zp], r_z.at[zp], head=z + 1)

    def down_copy(zp):
        return remote(ogf.at[zp], ogf.at[zp], s_dn.at[zp], r_z.at[zp], head=z - 1)

    def kv_copy(o):
        if o == 0:
            src, dst, to = kc.at[:, pl.ds(0, leaf)], 1, partner
        elif o % 2 == 0:
            level = o.bit_length() - 1
            src = pb.at[:, pl.ds(leaf - (leaf >> (level - 1)), rows[o])]
            dst, to = o, flipped(me, o)
        else:
            src, dst, to = kc.at[:, pl.ds(starts[o - 1], rows[o])], o, partner
        slot = kc.at[:, pl.ds(starts[dst], rows[dst])]
        return remote(src, slot, s_kv.at[o], r_kv.at[dst], seq=to)

    def kv_arrived(o):
        arrived(kc.at[:, pl.ds(starts[o], rows[o])], r_kv.at[o])

    def a_copy(zp, j):
        to = zp * per_shard + j
        return remote(ogf.at[zp, :, pl.ds(j * kcols, kcols)], ogs.at[me],
                      s_a.at[to], r_a.at[me], seq=to)

    def c_copy(o):
        if o == 1 or o % 2 == 0:
            return remote(ctxs.at[0], ctxs.at[o], s_c.at[o], r_c.at[o], seq=flipped(me, o))
        return remote(ctxs.at[o - 1], ctxs.at[o], s_c.at[o], r_c.at[o], seq=partner)

    def p_copy(g):
        return remote(dbuf.at[g, :, pl.ds(half, half)], pair.at[g], s_p.at[g], r_p.at[g],
                      seq=partner)

    def g_copy(g, o):
        return remote(dbuf.at[g, :, pl.ds(starts[o], rows[o])],
                      back.at[g, :, pl.ds(starts[o] - leaf, rows[o])],
                      s_g.at[g, o // 2], r_g.at[g, o // 2], seq=flipped(me, o))

    far = list(range(2, seq_count, 2))

    for zp in range(head_count):
        w_copy(zp).start()
    barrier = pltpu.get_barrier_semaphore()
    for o in range(1, seq_count):
        pl.semaphore_signal(barrier, inc=1, device_id={"seq": flipped(me, o)},
                            device_id_type=pl.DeviceIdType.MESH)

    @pl.when(z > 0)
    def _():
        pl.semaphore_signal(barrier, inc=1, device_id={"head": z - 1},
                            device_id_type=pl.DeviceIdType.MESH)

    @pl.when(z < head_count - 1)
    def _():
        pl.semaphore_signal(barrier, inc=1, device_id={"head": z + 1},
                            device_id_type=pl.DeviceIdType.MESH)

    ogf[z] = og_ref[...]
    kc[0, 0:leaf] = k_ref[...]
    kc[1, 0:leaf] = v_ref[...]
    for which, ref in enumerate((k_ref, v_ref)):
        for c in range(0, feats, 256):
            block = ref[:, c:c + 256]
            at = 0
            for level in range(1, levels):
                n = leaf >> level
                pool = jnp.where(
                    lax.broadcasted_iota(jnp.int32, (n, 2 * n), 1) // 2
                    == lax.broadcasted_iota(jnp.int32, (n, 2 * n), 0), 0.5, 0.0).astype(BF16)
                block = dot_nn(pool, block).astype(BF16)
                pb[which, at:at + n, c:c + 256] = block
                at += n
    inner = (z > 0) & (z < head_count - 1)

    @pl.when(inner)
    def _():
        pl.semaphore_wait(barrier, seq_count + 1)

    @pl.when(jnp.logical_not(inner))
    def _():
        pl.semaphore_wait(barrier, seq_count)

    @pl.when(z > 0)
    def _():
        down_copy(z).start()

    @pl.when(z < head_count - 1)
    def _():
        up_copy(z).start()

    kv_copy(0).start()
    for o in far:
        kv_copy(o).start()

    def scatter_grad(zp):
        for j in range(per_shard):
            @pl.when(zp * per_shard + j != me)
            def _():
                a_copy(zp, j).start()

            @pl.when(zp * per_shard + j == me)
            def _():
                ogs[me] = ogf[zp, :, j * kcols:(j + 1) * kcols]

    def project(zp, first=False):
        grad = ogf[zp]

        @pl.loop(0, feats // 256)
        def _(t):
            at = pl.ds(pl.multiple_of(t * 256, 256), 256)
            term = dot_nt(wv[zp, at], grad)
            cga[at] = term if first else cga[at] + term

    def gather_step(k):
        @pl.when(z >= k)
        def _():
            zp = z - k
            arrived(ogf.at[zp], r_z.at[zp])

            @pl.when(z < head_count - 1)
            def _():
                up_copy(zp).start()

        @pl.when(z + k < head_count)
        def _():
            zp = z + k
            arrived(ogf.at[zp], r_z.at[zp])

            @pl.when(z > 0)
            def _():
                down_copy(zp).start()

        @pl.when(z >= k)
        def _():
            scatter_grad(z - k)
            project(z - k)

        @pl.when(z + k < head_count)
        def _():
            scatter_grad(z + k)
            project(z + k)

    scatter_grad(z)
    for zp in range(head_count):
        w_copy(zp).wait()
    project(z, first=True)
    gather_step(1)

    for o in far:
        kv_arrived(o)
        kv_copy(o + 1).start()
    kv_arrived(1)
    for o in far:
        kv_arrived(o + 1)

    log2e = 1.4426950408889634
    my_doc = doc[0, me]
    biases = []
    for o in sorted(starts, key=lambda p: starts[p]):
        level = float(max(o.bit_length() - 1, 0))
        same = doc[0, flipped(me, o)] == my_doc
        biases.append((starts[o], rows[o], jnp.where(same, level, -1e30).astype(F32)))

    def forward(first, last):
        @pl.loop(first, last)
        def _(h):
            at = pl.ds(pl.multiple_of(h * DH, DH), DH)
            keys, vals, query = kc[0, :, at], kc[1, :, at], q_ref[:, at]
            raw = dot_nt(keys, query)
            shifted = jnp.concatenate(
                [raw[s:s + n] * (scaling * log2e) + b for s, n, b in biases], axis=0)
            top = jnp.max(shifted, axis=0, keepdims=True)
            weights = jnp.exp2(shifted - top)
            inv = 1.0 / jnp.sum(weights, axis=0, keepdims=True)
            prob = (weights * inv).astype(BF16)
            probs[h] = prob
            out = dot_tn(vals, prob)
            ctxs[0, at] = out.astype(BF16)
            ctx_out[:, at] = out.T.astype(BF16)

    forward(0, heads // 2)
    if head_count > 2:
        gather_step(2)
    forward(heads // 2, heads)
    for o in far + [1]:
        c_copy(o).start()
    for k in range(3, head_count):
        gather_step(k)
    cgt[...] = cga[...].astype(BF16)

    def finish(g):
        arrived(pair.at[g], r_p.at[g])
        for which in range(2):
            dbuf[g, which, leaf:half] = (
                dbuf[g, which, leaf:half].astype(F32) + pair[g, which, leaf:half].astype(F32)
            ).astype(BF16)
        for o in far:
            g_copy(g, o).start()

    @pl.loop(0, groups)
    def _(g):
        for i in range(GROUP_HEADS):
            h = g * GROUP_HEADS + i
            at = pl.ds(pl.multiple_of(h * DH, DH), DH)
            lanes = slice(i * DH, (i + 1) * DH)
            keys, vals, query = kc[0, :, at], kc[1, :, at], q_ref[:, at]
            grad = cgt[at]
            prob = probs[h]
            delta = jnp.sum(grad.astype(F32) * ctxs[0, at].astype(F32), axis=0, keepdims=True)
            prob_grad = dot_nn(vals, grad)
            score_grad = (prob.astype(F32) * (prob_grad - delta)).astype(BF16)
            dq_out[:, at] = (dot_tn(keys, score_grad) * scaling).T.astype(BF16)
            dk = dot_nn(score_grad, query) * scaling
            dv = dot_nt(prob, grad)
            for which, full in enumerate((dk, dv)):
                own[g, which, :, lanes] = full[:leaf]
                dbuf[g, which, leaf:, lanes] = full[leaf:].astype(BF16)
        p_copy(g).start()

        @pl.when(g > 0)
        def _():
            finish(g - 1)

    finish(groups - 1)

    for o in far:
        arrived(ctxs.at[o], r_c.at[o])
        c_copy(o + 1).start()
    for n, o in enumerate([0, 1] + far + [o + 1 for o in far]):
        if o % 2 == 1:
            arrived(ctxs.at[o], r_c.at[o])
        src = flipped(me, o)
        if o:
            arrived(ogs.at[src], r_a.at[src])
        grad = ogs[src]

        @pl.loop(0, feats // 256)
        def _(t):
            at = pl.ds(pl.multiple_of(t * 256, 256), 256)
            term = dot_nn(ctxs[o, at], grad)
            acc[at] = term if n == 0 else acc[at] + term

    wg_out[...] = acc[...].astype(BF16)

    far_rows = half - leaf
    r_id = lax.broadcasted_iota(jnp.int32, (leaf, far_rows), 0)
    c_id = lax.broadcasted_iota(jnp.int32, (leaf, far_rows), 1)
    spread = jnp.zeros((leaf, far_rows), F32)
    for o in far:
        level = o.bit_length() - 1
        hit = (lax.shift_right_logical(r_id, level) == c_id - (starts[o] - leaf))
        spread = jnp.where(hit, 0.5 ** level, spread)
    spread = spread.astype(BF16)
    for g in range(groups):
        for o in far:
            arrived(back.at[g, :, pl.ds(starts[o] - leaf, rows[o])], r_g.at[g, o // 2])
        for which, out in enumerate((dk_out, dv_out)):
            total = own[g, which] + pair[g, which, :leaf].astype(F32) + dot_nn(
                spread, back[g, which])
            out[:, g * gcols:(g + 1) * gcols] = total.astype(BF16)

    for zp in range(head_count):
        @pl.when((z < head_count - 1) & (zp <= z))
        def _():
            up_copy(zp).wait_send()

        @pl.when((z > 0) & (zp >= z))
        def _():
            down_copy(zp).wait_send()

        for j in range(per_shard):
            @pl.when(zp * per_shard + j != me)
            def _():
                a_copy(zp, j).wait_send()
    kv_copy(0).wait_send()
    for o in far:
        kv_copy(o).wait_send()
        kv_copy(o + 1).wait_send()
    for o in range(1, seq_count):
        c_copy(o).wait_send()
    for g in range(groups):
        p_copy(g).wait_send()
        for o in far:
            g_copy(g, o).wait_send()


def local(queries, keys, values, out_weight, out_grad, block_doc):
    seq_count, head_count = lax.axis_size("seq"), lax.axis_size("head")
    _, leaf, feats = queries.shape
    model = out_weight.shape[1]
    _, _, cols = pieces_of(seq_count, leaf)
    half = cols // 2
    heads = feats // DH
    gcols = GROUP_HEADS * DH
    groups = feats // gcols
    kcols = model // seq_count
    dma = pltpu.SemaphoreType.DMA
    vmem = pl.BlockSpec(memory_space=pltpu.VMEM)
    block = jax.ShapeDtypeStruct((leaf, feats), BF16)
    results = pl.pallas_call(
        functools.partial(kernel, seq_count, head_count, leaf, feats),
        out_shape=[block] * 4 + [jax.ShapeDtypeStruct((feats, kcols), BF16)],
        in_specs=[pl.BlockSpec(memory_space=pltpu.SMEM)] + [vmem] * 4
        + [pl.BlockSpec(memory_space=pl.ANY)],
        out_specs=[vmem] * 5,
        scratch_shapes=[
            pltpu.VMEM((head_count, feats, feats), BF16),
            pltpu.VMEM((head_count, leaf, feats), BF16),
            pltpu.VMEM((2, cols, feats), BF16),
            pltpu.VMEM((2, leaf, feats), BF16),
            pltpu.VMEM((heads, cols, leaf), BF16),
            pltpu.VMEM((seq_count, feats, leaf), BF16),
            pltpu.VMEM((seq_count, leaf, kcols), BF16),
            pltpu.VMEM((feats, leaf), F32),
            pltpu.VMEM((feats, leaf), BF16),
            pltpu.VMEM((groups, 2, leaf, gcols), F32),
            pltpu.VMEM((groups, 2, cols, gcols), BF16),
            pltpu.VMEM((groups, 2, half, gcols), BF16),
            pltpu.VMEM((groups, 2, half - leaf, gcols), BF16),
            pltpu.VMEM((feats, kcols), F32),
            dma((head_count,)), dma((head_count,)), dma((head_count,)), dma((head_count,)),
            dma((seq_count,)), dma((seq_count,)), dma((seq_count,)), dma((seq_count,)),
            dma((seq_count,)), dma((seq_count,)), dma((groups,)), dma((groups,)),
            dma((groups, seq_count // 2)), dma((groups, seq_count // 2)),
        ],
        compiler_params=pltpu.CompilerParams(
            collective_id=0, has_side_effects=True, vmem_limit_bytes=60 * 1024 * 1024),
        cost_estimate=pl.CostEstimate(
            flops=8 * 10**9, bytes_accessed=16 * 2**20, transcendentals=2 * 2**20),
        name="hier_attention",
    )(block_doc, queries[0], keys[0], values[0], out_grad[0], out_weight)
    context, query_grad, key_grad, value_grad, weight_grad = results
    return context[None], query_grad[None], key_grad[None], value_grad[None], weight_grad


def solution(mesh):
    blocks = P(None, "seq", "head")
    return jax.shard_map(
        local,
        mesh=mesh,
        in_specs=(blocks, blocks, blocks, P("head", None), blocks, P()),
        out_specs=(blocks, blocks, blocks, blocks, P("head", "seq")),
        check_vma=False,
    )
```

profile of v0, /device:TPU:25, one launch (start us, length us, event | category | flops | bytes accessed | tf_op | source)
XLA Modules:
  0.0 105.8 jit_solution(5239370497485474803)
XLA Ops:
  0.6 95.5 %hier_attention.1 = (bf16[256,1024]{1,0:T(8,128)(2,1)}, bf16[256,1024]{1,0:T(8,128)(2,1)}, bf16[256,1024]{1,0:T(8,128)(2,1)}, bf16[256,1024]{1,0:T(8,128)(2,1)}, bf16[1024,512]{1,0:T(8,128)(2,1)}) custom-call(s32[1,8]{1,0:T(1,128)} %doc.1, bf16[256,1024]{1,0:T(8,128)(2,1)} %bitcast.12, bf16[256,1024]{1,0:T(8,128)(2,1)} %bitcast.13, ...), custom_call_target="tpu_custom_call" | custom-call | flops 8000000000 | bytes 16777216 | tf_op jit(solution)/shard_map/hier_attention/pallas_call | solution.py:380
  96.1 1.9 %copy.16 = bf16[1,256,1024]{2,1,0:T(8,128)(2,1)} copy(bf16[1,256,1024]{2,1,0:T(8,128)(2,1)} %bitcast.11) | data formatting | bytes 1048576
  98.0 1.9 %copy.17 = bf16[1,256,1024]{2,1,0:T(8,128)(2,1)} copy(bf16[1,256,1024]{2,1,0:T(8,128)(2,1)} %bitcast.10) | data formatting | bytes 1048576
  99.9 1.9 %copy.18 = bf16[1,256,1024]{2,1,0:T(8,128)(2,1)} copy(bf16[1,256,1024]{2,1,0:T(8,128)(2,1)} %bitcast.9) | data formatting | bytes 1048576
  101.7 1.9 %copy.19 = bf16[1,256,1024]{2,1,0:T(8,128)(2,1)} copy(bf16[1,256,1024]{2,1,0:T(8,128)(2,1)} %bitcast.8) | data formatting | bytes 1048576
  103.6 2.3 %copy.20 = bf16[1024,512]{1,0:T(8,128)(2,1)} copy(bf16[1024,512]{1,0:T(8,128)(2,1)} %get-tuple-element.24) | data formatting | bytes 2097152
where the time goes:
time: 106 us
  Pallas kernels  95.5 us (90%)
  local copies, waits for them, and re-layouts  9.73 us (9%)
    pallas_call x1, Pallas kernels, local(): pl.pallas_call(functools.partial(kernel, seq_count, head_count, leaf, fea...  95.5 us
    unnamed x5, local copies, waits for them, and re-layouts  9.73 us

commit v1 on v0

--- a/solution.py
+++ b/solution.py
@@ -22,6 +22,10 @@
             out = out + (1 - 2 * lax.rem(lax.div(index, jnp.int32(bit)), jnp.int32(2))) * bit
         bit *= 2
     return out
+
+
+def top_bit(o):
+    return 1 << (o.bit_length() - 1)
 
 
 def dot_nn(a, b):
@@ -86,9 +90,8 @@
         if o == 0:
             src, dst, to = kc.at[:, pl.ds(0, leaf)], 1, partner
         elif o % 2 == 0:
-            level = o.bit_length() - 1
-            src = pb.at[:, pl.ds(leaf - (leaf >> (level - 1)), rows[o])]
-            dst, to = o, flipped(me, o)
+            src = pb.at[:, pl.ds(starts[o] - leaf, rows[o])]
+            dst, to = o, flipped(me, top_bit(o))
         else:
             src, dst, to = kc.at[:, pl.ds(starts[o - 1], rows[o])], o, partner
         slot = kc.at[:, pl.ds(starts[dst], rows[dst])]
@@ -102,19 +105,35 @@
         return remote(ogf.at[zp, :, pl.ds(j * kcols, kcols)], ogs.at[me],
                       s_a.at[to], r_a.at[me], seq=to)
 
-    def c_copy(o):
-        if o == 1 or o % 2 == 0:
-            return remote(ctxs.at[0], ctxs.at[o], s_c.at[o], r_c.at[o], seq=flipped(me, o))
-        return remote(ctxs.at[o - 1], ctxs.at[o], s_c.at[o], r_c.at[o], seq=partner)
+    def c_parts(o):
+        return 1 if o % 2 == 1 or o == top_bit(o) else 2
+
+    def c_copy(o, n=0):
+        if o == top_bit(o):
+            src, dst, bit = ctxs.at[0], ctxs.at[o], o
+        elif o % 2 == 1:
+            src, dst, bit = ctxs.at[o - 1], ctxs.at[o], 1
+        else:
+            bit = o & -o if n else top_bit(o)
+            part = pl.ds(n * (feats // 2), feats // 2)
+            src, dst = ctxs.at[o ^ bit, part], ctxs.at[o, part]
+        return remote(src, dst, s_c.at[o, n], r_c.at[o, n], seq=flipped(me, bit))
+
+    def c_arrived(o):
+        for n in range(c_parts(o)):
+            c_copy(o, n).wait_recv()
 
     def p_copy(g):
         return remote(dbuf.at[g, :, pl.ds(half, half)], pair.at[g], s_p.at[g], r_p.at[g],
                       seq=partner)
 
-    def g_copy(g, o):
-        return remote(dbuf.at[g, :, pl.ds(starts[o], rows[o])],
-                      back.at[g, :, pl.ds(starts[o] - leaf, rows[o])],
-                      s_g.at[g, o // 2], r_g.at[g, o // 2], seq=flipped(me, o))
+    def level_rows(level):
+        return starts[1 << level], (leaf >> level) << (level - 1)
+
+    def g_copy(g, level):
+        at, n = level_rows(level)
+        return remote(dbuf.at[g, :, pl.ds(at, n)], back.at[g, level - 1],
+                      s_g.at[g, level - 1], r_g.at[g, level - 1], seq=flipped(me, 1 << level))
 
     far = list(range(2, seq_count, 2))
 
@@ -138,18 +157,22 @@
     ogf[z] = og_ref[...]
     kc[0, 0:leaf] = k_ref[...]
     kc[1, 0:leaf] = v_ref[...]
-    for which, ref in enumerate((k_ref, v_ref)):
-        for c in range(0, feats, 256):
-            block = ref[:, c:c + 256]
-            at = 0
-            for level in range(1, levels):
-                n = leaf >> level
-                pool = jnp.where(
-                    lax.broadcasted_iota(jnp.int32, (n, 2 * n), 1) // 2
-                    == lax.broadcasted_iota(jnp.int32, (n, 2 * n), 0), 0.5, 0.0).astype(BF16)
-                block = dot_nn(pool, block).astype(BF16)
-                pb[which, at:at + n, c:c + 256] = block
-                at += n
+
+    def pool_from(source, low, r):
+        for which in range(2):
+            for c in range(0, feats, 256):
+                piece = source(which, c)
+                for level in range(low + 1, levels):
+                    n = leaf >> level
+                    pool = jnp.where(
+                        lax.shift_right_logical(
+                            lax.broadcasted_iota(jnp.int32, (n, 2 * n), 1), 1)
+                        == lax.broadcasted_iota(jnp.int32, (n, 2 * n), 0), 0.5, 0.0).astype(BF16)
+                    piece = dot_nn(pool, piece).astype(BF16)
+                    at = starts[(1 << level) + r] - leaf
+                    pb[which, at:at + n, c:c + 256] = piece
+
+    pool_from(lambda which, c: (k_ref, v_ref)[which][:, c:c + 256], 0, 0)
     inner = (z > 0) & (z < head_count - 1)
 
     @pl.when(inner)
@@ -169,8 +192,8 @@
         up_copy(z).start()
 
     kv_copy(0).start()
-    for o in far:
-        kv_copy(o).start()
+    for level in range(1, levels):
+        kv_copy(1 << level).start()
 
     def scatter_grad(zp):
         for j in range(per_shard):
@@ -229,6 +252,12 @@
     for o in far:
         kv_arrived(o)
         kv_copy(o + 1).start()
+        low = o.bit_length() - 1
+        if low + 1 < levels:
+            pool_from(lambda which, c: kc[which, starts[o]:starts[o] + rows[o], c:c + 256],
+                      low, o)
+            for level in range(low + 1, levels):
+                kv_copy((1 << level) + o).start()
     kv_arrived(1)
     for o in far:
         kv_arrived(o + 1)
@@ -262,20 +291,45 @@
     if head_count > 2:
         gather_step(2)
     forward(heads // 2, heads)
-    for o in far + [1]:
-        c_copy(o).start()
+    for level in range(levels - 1, -1, -1):
+        c_copy(1 << level).start()
     for k in range(3, head_count):
         gather_step(k)
     cgt[...] = cga[...].astype(BF16)
 
-    def finish(g):
+    def spread_from(level):
+        at, n = level_rows(level)
+        row = lax.broadcasted_iota(jnp.int32, (at, n), 0)
+        col = lax.broadcasted_iota(jnp.int32, (at, n), 1)
+        out = jnp.zeros((at, n), F32)
+        for r in range(0, 1 << level, 2):
+            low = max(r.bit_length() - 1, 0)
+            first = starts[(1 << level) + r] - at
+            inside = (row >= starts[r]) & (row < starts[r] + rows[r])
+            hit = lax.shift_right_logical(row - starts[r], level - low) == col - first
+            out = jnp.where(inside & hit, 0.5 ** (level - low), out)
+        return out.astype(BF16)
+
+    def finish_pair(g):
         arrived(pair.at[g], r_p.at[g])
         for which in range(2):
+            own[g, which] += pair[g, which, :leaf].astype(F32)
             dbuf[g, which, leaf:half] = (
                 dbuf[g, which, leaf:half].astype(F32) + pair[g, which, leaf:half].astype(F32)
             ).astype(BF16)
-        for o in far:
-            g_copy(g, o).start()
+        g_copy(g, levels - 1).start()
+
+    def finish_level(g, level, spread):
+        at, n = level_rows(level)
+        arrived(back.at[g, level - 1], r_g.at[g, level - 1])
+        for which in range(2):
+            more = dot_nn(spread, back[g, level - 1, which])
+            own[g, which] += more[:leaf]
+            if at > leaf:
+                dbuf[g, which, leaf:at] = (
+                    dbuf[g, which, leaf:at].astype(F32) + more[leaf:]).astype(BF16)
+        if level > 1:
+            g_copy(g, level - 1).start()
 
     @pl.loop(0, groups)
     def _(g):
@@ -299,16 +353,17 @@
 
         @pl.when(g > 0)
         def _():
-            finish(g - 1)
-
-    finish(groups - 1)
-
-    for o in far:
-        arrived(ctxs.at[o], r_c.at[o])
-        c_copy(o + 1).start()
-    for n, o in enumerate([0, 1] + far + [o + 1 for o in far]):
-        if o % 2 == 1:
-            arrived(ctxs.at[o], r_c.at[o])
+            finish_pair(g - 1)
+
+    finish_pair(groups - 1)
+    for level in range(levels - 1, 1, -1):
+        spread = spread_from(level)
+
+        @pl.loop(0, groups)
+        def _(g):
+            finish_level(g, level, spread)
+
+    def add_weight(o, first=False):
         src = flipped(me, o)
         if o:
             arrived(ogs.at[src], r_a.at[src])
@@ -318,26 +373,35 @@
         def _(t):
             at = pl.ds(pl.multiple_of(t * 256, 256), 256)
             term = dot_nn(ctxs[o, at], grad)
-            acc[at] = term if n == 0 else acc[at] + term
+            acc[at] = term if first else acc[at] + term
+
+    for o in far:
+        c_arrived(o)
+        c_copy(o + 1).start()
+        for level in range(1, levels):
+            bit = 1 << level
+            if o & bit:
+                continue
+            to = o | bit
+            if bit == top_bit(to):
+                c_copy(to, 0).start()
+            if bit == to & -to:
+                c_copy(to, 1).start()
+    add_weight(0, first=True)
+    c_arrived(1)
+    add_weight(1)
+    for o in far:
+        add_weight(o)
+        c_arrived(o + 1)
+        add_weight(o + 1)
 
     wg_out[...] = acc[...].astype(BF16)
 
-    far_rows = half - leaf
-    r_id = lax.broadcasted_iota(jnp.int32, (leaf, far_rows), 0)
-    c_id = lax.broadcasted_iota(jnp.int32, (leaf, far_rows), 1)
-    spread = jnp.zeros((leaf, far_rows), F32)
-    for o in far:
-        level = o.bit_length() - 1
-        hit = (lax.shift_right_logical(r_id, level) == c_id - (starts[o] - leaf))
-        spread = jnp.where(hit, 0.5 ** level, spread)
-    spread = spread.astype(BF16)
+    last = spread_from(1)
     for g in range(groups):
-        for o in far:
-            arrived(back.at[g, :, pl.ds(starts[o] - leaf, rows[o])], r_g.at[g, o // 2])
+        finish_level(g, 1, last)
         for which, out in enumerate((dk_out, dv_out)):
-            total = own[g, which] + pair[g, which, :leaf].astype(F32) + dot_nn(
-                spread, back[g, which])
-            out[:, g * gcols:(g + 1) * gcols] = total.astype(BF16)
+            out[:, g * gcols:(g + 1) * gcols] = own[g, which].astype(BF16)
 
     for zp in range(head_count):
         @pl.when((z < head_count - 1) & (zp <= z))
@@ -357,11 +421,22 @@
         kv_copy(o).wait_send()
         kv_copy(o + 1).wait_send()
     for o in range(1, seq_count):
-        c_copy(o).wait_send()
+        for n in range(c_parts(o)):
+            c_copy(o, n).wait_send()
     for g in range(groups):
         p_copy(g).wait_send()
-        for o in far:
-            g_copy(g, o).wait_send()
+        for level in range(1, levels):
+            g_copy(g, level).wait_send()
+
+
+def copy_kernel(*refs):
+    count = len(refs) // 2
+    sems = refs[-1]
+    copies = [pltpu.make_async_copy(refs[i], refs[count + i], sems.at[i]) for i in range(count)]
+    for copy in copies:
+        copy.start()
+    for copy in copies:
+        copy.wait()
 
 
 def local(queries, keys, values, out_weight, out_grad, block_doc):
@@ -374,6 +449,7 @@
     gcols = GROUP_HEADS * DH
     groups = feats // gcols
     kcols = model // seq_count
+    levels = seq_count.bit_length() - 1
     dma = pltpu.SemaphoreType.DMA
     vmem = pl.BlockSpec(memory_space=pltpu.VMEM)
     block = jax.ShapeDtypeStruct((leaf, feats), BF16)
@@ -387,7 +463,7 @@
             pltpu.VMEM((head_count, feats, feats), BF16),
             pltpu.VMEM((head_count, leaf, feats), BF16),
             pltpu.VMEM((2, cols, feats), BF16),
-            pltpu.VMEM((2, leaf, feats), BF16),
+            pltpu.VMEM((2, half - leaf, feats), BF16),
             pltpu.VMEM((heads, cols, leaf), BF16),
             pltpu.VMEM((seq_count, feats, leaf), BF16),
             pltpu.VMEM((seq_count, leaf, kcols), BF16),
@@ -396,12 +472,12 @@
             pltpu.VMEM((groups, 2, leaf, gcols), F32),
             pltpu.VMEM((groups, 2, cols, gcols), BF16),
             pltpu.VMEM((groups, 2, half, gcols), BF16),
-            pltpu.VMEM((groups, 2, half - leaf, gcols), BF16),
+            pltpu.VMEM((groups, levels - 1, 2, leaf // 2, gcols), BF16),
             pltpu.VMEM((feats, kcols), F32),
             dma((head_count,)), dma((head_count,)), dma((head_count,)), dma((head_count,)),
             dma((seq_count,)), dma((seq_count,)), dma((seq_count,)), dma((seq_count,)),
-            dma((seq_count,)), dma((seq_count,)), dma((groups,)), dma((groups,)),
-            dma((groups, seq_count // 2)), dma((groups, seq_count // 2)),
+            dma((seq_count, 2)), dma((seq_count, 2)), dma((groups,)), dma((groups,)),
+            dma((groups, levels - 1)), dma((groups, levels - 1)),
         ],
         compiler_params=pltpu.CompilerParams(
             collective_id=0, has_side_effects=True, vmem_limit_bytes=60 * 1024 * 1024),
@@ -409,7 +485,16 @@
             flops=8 * 10**9, bytes_accessed=16 * 2**20, transcendentals=2 * 2**20),
         name="hier_attention",
     )(block_doc, queries[0], keys[0], values[0], out_grad[0], out_weight)
-    context, query_grad, key_grad, value_grad, weight_grad = results
+    anywhere = pl.BlockSpec(memory_space=pl.ANY)
+    context, query_grad, key_grad, value_grad, weight_grad = pl.pallas_call(
+        copy_kernel,
+        out_shape=[jax.ShapeDtypeStruct(r.shape, r.dtype) for r in results],
+        in_specs=[anywhere] * 5,
+        out_specs=[anywhere] * 5,
+        scratch_shapes=[dma((5,))],
+        compiler_params=pltpu.CompilerParams(vmem_limit_bytes=60 * 1024 * 1024),
+        name="hand_over",
+    )(*results)
     return context[None], query_grad[None], key_grad[None], value_grad[None], weight_grad
 
 

time: 106 us -> 223 us (2.10)
  the two profiles are of different devices: /device:TPU:25 before, /device:TPU:5 now
where the time goes in v1:
time: 223 us; the launch traced here: 222 us
  Pallas kernels  222 us (100%)
    pallas_call x1, Pallas kernels, local(): pl.pallas_call(functools.partial(kernel, seq_count, head_count, leaf, fea...  125 us
    pallas_call x1, Pallas kernels, local(): pl.pallas_call(copy_kernel, out_shape=[jax.ShapeDtypeStruct(r.shape, r.dt...  96.4 us

profile of v1, /device:TPU:5, one launch (start us, length us, event | category | flops | bytes accessed | tf_op | source)
XLA Modules:
  0.0 222.4 jit_solution(15476168032505548126)
XLA Ops:
  0.6 125.3 %hier_attention.1 = (bf16[256,1024]{1,0:T(8,128)(2,1)}, bf16[256,1024]{1,0:T(8,128)(2,1)}, bf16[256,1024]{1,0:T(8,128)(2,1)}, bf16[256,1024]{1,0:T(8,128)(2,1)}, bf16[1024,512]{1,0:T(8,128)(2,1)}) custom-call(s32[1,8]{1,0:T(1,128)} %doc.1, bf16[256,1024]{1,0:T(8,128)(2,1)} %bitcast.8, bf16[256,1024]{1,0:T(8,128)(2,1)} %bitcast.9, ...), custom_call_target="tpu_custom_call" | custom-call | flops 8000000000 | bytes 16777216 | tf_op jit(solution)/shard_map/hier_attention/pallas_call | solution.py:456
  126.0 96.4 %hand_over.1 = (bf16[256,1024]{1,0:T(8,128)(2,1)}, bf16[256,1024]{1,0:T(8,128)(2,1)}, bf16[256,1024]{1,0:T(8,128)(2,1)}, bf16[256,1024]{1,0:T(8,128)(2,1)}, bf16[1024,512]{1,0:T(8,128)(2,1)}) custom-call(bf16[256,1024]{1,0:T(8,128)(2,1)} %get-tuple-element.15.refs_0_, bf16[256,1024]{1,0:T(8,128)(2,1)} %get-tuple-element.16.refs_1_, ...), custom_call_target="tpu_custom_call" | custom-call | tf_op jit(solution)/shard_map/hand_over/pallas_call | solution.py:489

commit v2 on v1

--- a/solution.py
+++ b/solution.py
@@ -66,6 +66,7 @@
     groups = feats // gcols
     per_shard = seq_count // head_count
     kcols = feats // per_shard
+    hf = feats // 2
     scaling = 1.0 / math.sqrt(DH)
 
     def remote(src, dst, send, recv, **where):
@@ -80,48 +81,61 @@
         return pltpu.make_async_copy(
             w_ref.at[:, pl.ds(zp * feats, feats)], wv.at[zp], s_w.at[zp])
 
-    def up_copy(zp):
-        return remote(ogf.at[zp], ogf.at[zp], s_up.at[zp], r_z.at[zp], head=z + 1)
-
-    def down_copy(zp):
-        return remote(ogf.at[zp], ogf.at[zp], s_dn.at[zp], r_z.at[zp], head=z - 1)
-
-    def kv_copy(o):
+    def z_copy(zp, step, sem):
+        sems = s_up if step > 0 else s_dn
+        return remote(ogf.at[zp], ogf.at[zp], sems.at[sem], r_z.at[zp], head=z + step)
+
+    def own_sends(act):
+        for step in (1, 2):
+            @pl.when(z + step < head_count)
+            def _():
+                act(z_copy(z, step, head_count + step - 1))
+
+            @pl.when(z >= step)
+            def _():
+                act(z_copy(z, -step, head_count + step - 1))
+
+    def kv_slot(o, n):
+        return kc.at[:, pl.ds(starts[o], rows[o]), pl.ds(n * hf, hf)]
+
+    def kv_copy(o, n):
         if o == 0:
-            src, dst, to = kc.at[:, pl.ds(0, leaf)], 1, partner
+            src, dst, to = kv_slot(0, n), 1, partner
         elif o % 2 == 0:
-            src = pb.at[:, pl.ds(starts[o] - leaf, rows[o])]
+            src = pb.at[:, pl.ds(starts[o] - leaf, rows[o]), pl.ds(n * hf, hf)]
             dst, to = o, flipped(me, top_bit(o))
         else:
-            src, dst, to = kc.at[:, pl.ds(starts[o - 1], rows[o])], o, partner
-        slot = kc.at[:, pl.ds(starts[dst], rows[dst])]
-        return remote(src, slot, s_kv.at[o], r_kv.at[dst], seq=to)
-
-    def kv_arrived(o):
-        arrived(kc.at[:, pl.ds(starts[o], rows[o])], r_kv.at[o])
+            src, dst, to = kv_slot(o - 1, n), o, partner
+        return remote(src, kv_slot(dst, n), s_kv.at[o, n], r_kv.at[dst, n], seq=to)
+
+    def kv_arrived(o, n):
+        arrived(kv_slot(o, n), r_kv.at[o, n])
 
     def a_copy(zp, j):
         to = zp * per_shard + j
         return remote(ogf.at[zp, :, pl.ds(j * kcols, kcols)], ogs.at[me],
                       s_a.at[to], r_a.at[me], seq=to)
 
-    def c_parts(o):
-        return 1 if o % 2 == 1 or o == top_bit(o) else 2
-
-    def c_copy(o, n=0):
+    def c_copy(o, n):
         if o == top_bit(o):
-            src, dst, bit = ctxs.at[0], ctxs.at[o], o
+            src, bit = 0, o
         elif o % 2 == 1:
-            src, dst, bit = ctxs.at[o - 1], ctxs.at[o], 1
+            src, bit = o - 1, 1
         else:
             bit = o & -o if n else top_bit(o)
-            part = pl.ds(n * (feats // 2), feats // 2)
-            src, dst = ctxs.at[o ^ bit, part], ctxs.at[o, part]
-        return remote(src, dst, s_c.at[o, n], r_c.at[o, n], seq=flipped(me, bit))
-
-    def c_arrived(o):
-        for n in range(c_parts(o)):
-            c_copy(o, n).wait_recv()
+            src = o ^ bit
+        part = pl.ds(n * hf, hf)
+        return remote(ctxs.at[src, part], ctxs.at[o, part], s_c.at[o, n], r_c.at[o, n],
+                      seq=flipped(me, bit))
+
+    def c_pass(o, n):
+        c_copy(o, n).wait_recv()
+        c_copy(o + 1, n).start()
+        for level in range(1, levels):
+            bit = 1 << level
+            to = o | bit
+            if not o & bit and bit == (to & -to if n else top_bit(to)):
+                c_copy(to, n).start()
 
     def p_copy(g):
         return remote(dbuf.at[g, :, pl.ds(half, half)], pair.at[g], s_p.at[g], r_p.at[g],
@@ -144,23 +158,17 @@
         pl.semaphore_signal(barrier, inc=1, device_id={"seq": flipped(me, o)},
                             device_id_type=pl.DeviceIdType.MESH)
 
-    @pl.when(z > 0)
-    def _():
-        pl.semaphore_signal(barrier, inc=1, device_id={"head": z - 1},
-                            device_id_type=pl.DeviceIdType.MESH)
-
-    @pl.when(z < head_count - 1)
-    def _():
-        pl.semaphore_signal(barrier, inc=1, device_id={"head": z + 1},
+    for step in range(1, head_count):
+        pl.semaphore_signal(barrier, inc=1, device_id={"head": lax.rem(z + step, head_count)},
                             device_id_type=pl.DeviceIdType.MESH)
 
     ogf[z] = og_ref[...]
     kc[0, 0:leaf] = k_ref[...]
     kc[1, 0:leaf] = v_ref[...]
 
-    def pool_from(source, low, r):
+    def pool_from(source, low, r, n_half):
         for which in range(2):
-            for c in range(0, feats, 256):
+            for c in range(n_half * hf, n_half * hf + hf, 256):
                 piece = source(which, c)
                 for level in range(low + 1, levels):
                     n = leaf >> level
@@ -172,28 +180,15 @@
                     at = starts[(1 << level) + r] - leaf
                     pb[which, at:at + n, c:c + 256] = piece
 
-    pool_from(lambda which, c: (k_ref, v_ref)[which][:, c:c + 256], 0, 0)
-    inner = (z > 0) & (z < head_count - 1)
-
-    @pl.when(inner)
-    def _():
-        pl.semaphore_wait(barrier, seq_count + 1)
-
-    @pl.when(jnp.logical_not(inner))
-    def _():
-        pl.semaphore_wait(barrier, seq_count)
-
-    @pl.when(z > 0)
-    def _():
-        down_copy(z).start()
-
-    @pl.when(z < head_count - 1)
-    def _():
-        up_copy(z).start()
-
-    kv_copy(0).start()
-    for level in range(1, levels):
-        kv_copy(1 << level).start()
+    for n in range(2):
+        pool_from(lambda which, c: (k_ref, v_ref)[which][:, c:c + 256], 0, 0, n)
+    pl.semaphore_wait(barrier, seq_count - 1 + head_count - 1)
+
+    own_sends(lambda copy: copy.start())
+    for n in range(2):
+        for level in range(1, levels):
+            kv_copy(1 << level, n).start()
+        kv_copy(0, n).start()
 
     def scatter_grad(zp):
         for j in range(per_shard):
@@ -219,19 +214,19 @@
         def _():
             zp = z - k
             arrived(ogf.at[zp], r_z.at[zp])
-
-            @pl.when(z < head_count - 1)
-            def _():
-                up_copy(zp).start()
+            if k >= 2:
+                @pl.when(z < head_count - 1)
+                def _():
+                    z_copy(zp, 1, zp).start()
 
         @pl.when(z + k < head_count)
         def _():
             zp = z + k
             arrived(ogf.at[zp], r_z.at[zp])
-
-            @pl.when(z > 0)
-            def _():
-                down_copy(zp).start()
+            if k >= 2:
+                @pl.when(z > 0)
+                def _():
+                    z_copy(zp, -1, zp).start()
 
         @pl.when(z >= k)
         def _():
@@ -243,24 +238,24 @@
             scatter_grad(z + k)
             project(z + k)
 
-    scatter_grad(z)
+    def columns(n):
+        for o in far:
+            kv_arrived(o, n)
+            kv_copy(o + 1, n).start()
+            low = o.bit_length() - 1
+            if low + 1 < levels:
+                pool_from(
+                    lambda which, c: kc[which, starts[o]:starts[o] + rows[o], c:c + 256],
+                    low, o, n)
+                for level in range(low + 1, levels):
+                    kv_copy((1 << level) + o, n).start()
+        kv_arrived(1, n)
+        for o in far:
+            kv_arrived(o + 1, n)
+
     for zp in range(head_count):
         w_copy(zp).wait()
     project(z, first=True)
-    gather_step(1)
-
-    for o in far:
-        kv_arrived(o)
-        kv_copy(o + 1).start()
-        low = o.bit_length() - 1
-        if low + 1 < levels:
-            pool_from(lambda which, c: kc[which, starts[o]:starts[o] + rows[o], c:c + 256],
-                      low, o)
-            for level in range(low + 1, levels):
-                kv_copy((1 << level) + o).start()
-    kv_arrived(1)
-    for o in far:
-        kv_arrived(o + 1)
 
     log2e = 1.4426950408889634
     my_doc = doc[0, me]
@@ -287,14 +282,23 @@
             ctxs[0, at] = out.astype(BF16)
             ctx_out[:, at] = out.T.astype(BF16)
 
+    def send_context(n):
+        for level in range(levels - 1, -1, -1):
+            c_copy(1 << level, n).start()
+
+    columns(0)
     forward(0, heads // 2)
-    if head_count > 2:
-        gather_step(2)
+    send_context(0)
+    columns(1)
+    scatter_grad(z)
     forward(heads // 2, heads)
-    for level in range(levels - 1, -1, -1):
-        c_copy(1 << level).start()
-    for k in range(3, head_count):
+    send_context(1)
+    gather_step(1)
+    for k in range(2, head_count - 1):
         gather_step(k)
+    for o in far:
+        c_pass(o, 0)
+    gather_step(head_count - 1)
     cgt[...] = cga[...].astype(BF16)
 
     def spread_from(level):
@@ -330,6 +334,20 @@
                     dbuf[g, which, leaf:at].astype(F32) + more[leaf:]).astype(BF16)
         if level > 1:
             g_copy(g, level - 1).start()
+
+    top_spread = spread_from(levels - 1)
+
+    def add_weight(o, first=False):
+        src = flipped(me, o)
+        if o:
+            arrived(ogs.at[src], r_a.at[src])
+        grad = ogs[src]
+
+        @pl.loop(0, feats // 256)
+        def _(t):
+            at = pl.ds(pl.multiple_of(t * 256, 256), 256)
+            term = dot_nn(ctxs[o, at], grad)
+            acc[at] = term if first else acc[at] + term
 
     @pl.loop(0, groups)
     def _(g):
@@ -355,44 +373,36 @@
         def _():
             finish_pair(g - 1)
 
+        if levels > 2:
+            @pl.when(g > 1)
+            def _():
+                finish_level(g - 2, levels - 1, top_spread)
+
+        @pl.when(g == groups // 2)
+        def _():
+            for level in range(1, levels):
+                c_pass(1 << level, 1)
+
     finish_pair(groups - 1)
+    for o in far:
+        if o != top_bit(o):
+            c_pass(o, 1)
+    add_weight(0, first=True)
     for level in range(levels - 1, 1, -1):
         spread = spread_from(level)
 
-        @pl.loop(0, groups)
+        @pl.loop(max(groups - 2, 0) if level == levels - 1 else 0, groups)
         def _(g):
             finish_level(g, level, spread)
 
-    def add_weight(o, first=False):
-        src = flipped(me, o)
-        if o:
-            arrived(ogs.at[src], r_a.at[src])
-        grad = ogs[src]
-
-        @pl.loop(0, feats // 256)
-        def _(t):
-            at = pl.ds(pl.multiple_of(t * 256, 256), 256)
-            term = dot_nn(ctxs[o, at], grad)
-            acc[at] = term if first else acc[at] + term
-
-    for o in far:
-        c_arrived(o)
-        c_copy(o + 1).start()
-        for level in range(1, levels):
-            bit = 1 << level
-            if o & bit:
-                continue
-            to = o | bit
-            if bit == top_bit(to):
-                c_copy(to, 0).start()
-            if bit == to & -to:
-                c_copy(to, 1).start()
-    add_weight(0, first=True)
-    c_arrived(1)
+    for n in range(2):
+        c_copy(1, n).wait_recv()
     add_weight(1)
     for o in far:
         add_weight(o)
-        c_arrived(o + 1)
+    for o in far:
+        for n in range(2):
+            c_copy(o + 1, n).wait_recv()
         add_weight(o + 1)
 
     wg_out[...] = acc[...].astype(BF16)
@@ -403,25 +413,26 @@
         for which, out in enumerate((dk_out, dv_out)):
             out[:, g * gcols:(g + 1) * gcols] = own[g, which].astype(BF16)
 
+    own_sends(lambda copy: copy.wait_send())
     for zp in range(head_count):
-        @pl.when((z < head_count - 1) & (zp <= z))
-        def _():
-            up_copy(zp).wait_send()
-
-        @pl.when((z > 0) & (zp >= z))
-        def _():
-            down_copy(zp).wait_send()
+        @pl.when((z < head_count - 1) & (z - zp >= 2))
+        def _():
+            z_copy(zp, 1, zp).wait_send()
+
+        @pl.when((z > 0) & (zp - z >= 2))
+        def _():
+            z_copy(zp, -1, zp).wait_send()
 
         for j in range(per_shard):
             @pl.when(zp * per_shard + j != me)
             def _():
                 a_copy(zp, j).wait_send()
-    kv_copy(0).wait_send()
-    for o in far:
-        kv_copy(o).wait_send()
-        kv_copy(o + 1).wait_send()
-    for o in range(1, seq_count):
-        for n in range(c_parts(o)):
+    for n in range(2):
+        kv_copy(0, n).wait_send()
+        for o in far:
+            kv_copy(o, n).wait_send()
+            kv_copy(o + 1, n).wait_send()
+        for o in range(1, seq_count):
             c_copy(o, n).wait_send()
     for g in range(groups):
         p_copy(g).wait_send()
@@ -431,12 +442,8 @@
 
 def copy_kernel(*refs):
     count = len(refs) // 2
-    sems = refs[-1]
-    copies = [pltpu.make_async_copy(refs[i], refs[count + i], sems.at[i]) for i in range(count)]
-    for copy in copies:
-        copy.start()
-    for copy in copies:
-        copy.wait()
+    for i in range(count):
+        refs[count + i][...] = refs[i][...]
 
 
 def local(queries, keys, values, out_weight, out_grad, block_doc):
@@ -474,8 +481,9 @@
             pltpu.VMEM((groups, 2, half, gcols), BF16),
             pltpu.VMEM((groups, levels - 1, 2, leaf // 2, gcols), BF16),
             pltpu.VMEM((feats, kcols), F32),
-            dma((head_count,)), dma((head_count,)), dma((head_count,)), dma((head_count,)),
-            dma((seq_count,)), dma((seq_count,)), dma((seq_count,)), dma((seq_count,)),
+            dma((head_count,)), dma((head_count + 2,)), dma((head_count + 2,)),
+            dma((head_count,)), dma((seq_count, 2)), dma((seq_count, 2)),
+            dma((seq_count,)), dma((seq_count,)),
             dma((seq_count, 2)), dma((seq_count, 2)), dma((groups,)), dma((groups,)),
             dma((groups, levels - 1)), dma((groups, levels - 1)),
         ],
@@ -485,13 +493,14 @@
             flops=8 * 10**9, bytes_accessed=16 * 2**20, transcendentals=2 * 2**20),
         name="hier_attention",
     )(block_doc, queries[0], keys[0], values[0], out_grad[0], out_weight)
-    anywhere = pl.BlockSpec(memory_space=pl.ANY)
+    steps = 4
+    tiles = [pl.BlockSpec((r.shape[0] // steps, r.shape[1]), lambda i: (i, 0)) for r in results]
     context, query_grad, key_grad, value_grad, weight_grad = pl.pallas_call(
         copy_kernel,
+        grid=(steps,),
         out_shape=[jax.ShapeDtypeStruct(r.shape, r.dtype) for r in results],
-        in_specs=[anywhere] * 5,
-        out_specs=[anywhere] * 5,
-        scratch_shapes=[dma((5,))],
+        in_specs=tiles,
+        out_specs=tiles,
         compiler_params=pltpu.CompilerParams(vmem_limit_bytes=60 * 1024 * 1024),
         name="hand_over",
     )(*results)

time: 223 us -> 125 us (0.56)
  the two profiles are of different devices: /device:TPU:5 before, /device:TPU:4 now
where the time goes in v2:
time: 125 us
  Pallas kernels  124 us (99%)
    pallas_call x1, Pallas kernels, local(): pl.pallas_call(functools.partial(kernel, seq_count, head_count, leaf, fea...  120 us
    pallas_call x1, Pallas kernels, local(): pl.pallas_call(copy_kernel, grid=(steps,), out_shape=[jax.ShapeDtypeStruc...  4.25 us

profile of v2, /device:TPU:4, one launch (start us, length us, event | category | flops | bytes accessed | tf_op | source)
XLA Modules:
  0.0 124.8 jit_solution(17936442143997269411)
XLA Ops:
  0.6 120.0 %hier_attention.1 = (bf16[256,1024]{1,0:T(8,128)(2,1)}, bf16[256,1024]{1,0:T(8,128)(2,1)}, bf16[256,1024]{1,0:T(8,128)(2,1)}, bf16[256,1024]{1,0:T(8,128)(2,1)}, bf16[1024,512]{1,0:T(8,128)(2,1)}) custom-call(s32[1,8]{1,0:T(1,128)} %doc.1, bf16[256,1024]{1,0:T(8,128)(2,1)} %bitcast.8, bf16[256,1024]{1,0:T(8,128)(2,1)} %bitcast.9, ...), custom_call_target="tpu_custom_call" | custom-call | flops 8000000000 | bytes 16777216 | tf_op jit(solution)/shard_map/hier_attention/pallas_call | solution.py:463
  120.6 4.2 %hand_over.1 = (bf16[256,1024]{1,0:T(8,128)(2,1)}, bf16[256,1024]{1,0:T(8,128)(2,1)}, bf16[256,1024]{1,0:T(8,128)(2,1)}, bf16[256,1024]{1,0:T(8,128)(2,1)}, bf16[1024,512]{1,0:T(8,128)(2,1)}) custom-call(bf16[256,1024]{1,0:T(8,128)(2,1)} %get-tuple-element.15.refs_0_, bf16[256,1024]{1,0:T(8,128)(2,1)} %get-tuple-element.16.refs_1_, ...), custom_call_target="tpu_custom_call" | custom-call | tf_op jit(solution)/shard_map/hand_over/pallas_call | solution.py:498

commit v3 on v0

--- a/solution.py
+++ b/solution.py
@@ -102,10 +102,10 @@
         return remote(ogf.at[zp, :, pl.ds(j * kcols, kcols)], ogs.at[me],
                       s_a.at[to], r_a.at[me], seq=to)
 
-    def c_copy(o):
-        if o == 1 or o % 2 == 0:
-            return remote(ctxs.at[0], ctxs.at[o], s_c.at[o], r_c.at[o], seq=flipped(me, o))
-        return remote(ctxs.at[o - 1], ctxs.at[o], s_c.at[o], r_c.at[o], seq=partner)
+    def c_copy(o, n):
+        part = pl.ds(n * (feats // 2), feats // 2)
+        src, to = (0, flipped(me, o)) if o == 1 or o % 2 == 0 else (o - 1, partner)
+        return remote(ctxs.at[src, part], ctxs.at[o, part], s_c.at[o, n], r_c.at[o, n], seq=to)
 
     def p_copy(g):
         return remote(dbuf.at[g, :, pl.ds(half, half)], pair.at[g], s_p.at[g], r_p.at[g],
@@ -212,15 +212,16 @@
 
         @pl.when(z >= k)
         def _():
-            scatter_grad(z - k)
+            if k > 1:
+                scatter_grad(z - k)
             project(z - k)
 
         @pl.when(z + k < head_count)
         def _():
-            scatter_grad(z + k)
+            if k > 1:
+                scatter_grad(z + k)
             project(z + k)
 
-    scatter_grad(z)
     for zp in range(head_count):
         w_copy(zp).wait()
     project(z, first=True)
@@ -232,6 +233,15 @@
     kv_arrived(1)
     for o in far:
         kv_arrived(o + 1)
+    scatter_grad(z)
+
+    @pl.when(z >= 1)
+    def _():
+        scatter_grad(z - 1)
+
+    @pl.when(z + 1 < head_count)
+    def _():
+        scatter_grad(z + 1)
 
     log2e = 1.4426950408889634
     my_doc = doc[0, me]
@@ -259,11 +269,13 @@
             ctx_out[:, at] = out.T.astype(BF16)
 
     forward(0, heads // 2)
+    for o in far + [1]:
+        c_copy(o, 0).start()
     if head_count > 2:
         gather_step(2)
     forward(heads // 2, heads)
     for o in far + [1]:
-        c_copy(o).start()
+        c_copy(o, 1).start()
     for k in range(3, head_count):
         gather_step(k)
     cgt[...] = cga[...].astype(BF16)
@@ -304,11 +316,13 @@
     finish(groups - 1)
 
     for o in far:
-        arrived(ctxs.at[o], r_c.at[o])
-        c_copy(o + 1).start()
+        for n in range(2):
+            c_copy(o, n).wait_recv()
+            c_copy(o + 1, n).start()
     for n, o in enumerate([0, 1] + far + [o + 1 for o in far]):
         if o % 2 == 1:
-            arrived(ctxs.at[o], r_c.at[o])
+            for n in range(2):
+                c_copy(o, n).wait_recv()
         src = flipped(me, o)
         if o:
             arrived(ogs.at[src], r_a.at[src])
@@ -357,11 +371,18 @@
         kv_copy(o).wait_send()
         kv_copy(o + 1).wait_send()
     for o in range(1, seq_count):
-        c_copy(o).wait_send()
+        for n in range(2):
+            c_copy(o, n).wait_send()
     for g in range(groups):
         p_copy(g).wait_send()
         for o in far:
             g_copy(g, o).wait_send()
+
+
+def copy_kernel(*refs):
+    count = len(refs) // 2
+    for i in range(count):
+        refs[count + i][...] = refs[i][...]
 
 
 def local(queries, keys, values, out_weight, out_grad, block_doc):
@@ -400,7 +421,7 @@
             pltpu.VMEM((feats, kcols), F32),
             dma((head_count,)), dma((head_count,)), dma((head_count,)), dma((head_count,)),
             dma((seq_count,)), dma((seq_count,)), dma((seq_count,)), dma((seq_count,)),
-            dma((seq_count,)), dma((seq_count,)), dma((groups,)), dma((groups,)),
+            dma((seq_count, 2)), dma((seq_count, 2)), dma((groups,)), dma((groups,)),
             dma((groups, seq_count // 2)), dma((groups, seq_count // 2)),
         ],
         compiler_params=pltpu.CompilerParams(
@@ -409,7 +430,17 @@
             flops=8 * 10**9, bytes_accessed=16 * 2**20, transcendentals=2 * 2**20),
         name="hier_attention",
     )(block_doc, queries[0], keys[0], values[0], out_grad[0], out_weight)
-    context, query_grad, key_grad, value_grad, weight_grad = results
+    steps = 4
+    tiles = [pl.BlockSpec((r.shape[0] // steps, r.shape[1]), lambda i: (i, 0)) for r in results]
+    context, query_grad, key_grad, value_grad, weight_grad = pl.pallas_call(
+        copy_kernel,
+        grid=(steps,),
+        out_shape=[jax.ShapeDtypeStruct(r.shape, r.dtype) for r in results],
+        in_specs=tiles,
+        out_specs=tiles,
+        compiler_params=pltpu.CompilerParams(vmem_limit_bytes=60 * 1024 * 1024),
+        name="hand_over",
+    )(*results)
     return context[None], query_grad[None], key_grad[None], value_grad[None], weight_grad
 
 

time: 106 us -> 98.4 us (0.928)
  the two profiles are of different devices: /device:TPU:25 before, /device:TPU:0 now
where the time goes in v3:
time: 98.4 us; the launch traced here: 98.2 us
  Pallas kernels  97.6 us (99%)
    pallas_call x1, Pallas kernels, local(): pl.pallas_call(functools.partial(kernel, seq_count, head_count, leaf, fea...  93.3 us
    pallas_call x1, Pallas kernels, local(): pl.pallas_call(copy_kernel, grid=(steps,), out_shape=[jax.ShapeDtypeStruc...  4.25 us

profile of v3, /device:TPU:0, one launch (start us, length us, event | category | flops | bytes accessed | tf_op | source)
XLA Modules:
  0.0 98.2 jit_solution(9418653205817172801)
XLA Ops:
  0.6 93.3 %hier_attention.1 = (bf16[256,1024]{1,0:T(8,128)(2,1)}, bf16[256,1024]{1,0:T(8,128)(2,1)}, bf16[256,1024]{1,0:T(8,128)(2,1)}, bf16[256,1024]{1,0:T(8,128)(2,1)}, bf16[1024,512]{1,0:T(8,128)(2,1)}) custom-call(s32[1,8]{1,0:T(1,128)} %doc.1, bf16[256,1024]{1,0:T(8,128)(2,1)} %bitcast.8, bf16[256,1024]{1,0:T(8,128)(2,1)} %bitcast.9, ...), custom_call_target="tpu_custom_call" | custom-call | flops 8000000000 | bytes 16777216 | tf_op jit(solution)/shard_map/hier_attention/pallas_call | solution.py:401
  93.9 4.2 %hand_over.1 = (bf16[256,1024]{1,0:T(8,128)(2,1)}, bf16[256,1024]{1,0:T(8,128)(2,1)}, bf16[256,1024]{1,0:T(8,128)(2,1)}, bf16[256,1024]{1,0:T(8,128)(2,1)}, bf16[1024,512]{1,0:T(8,128)(2,1)}) custom-call(bf16[256,1024]{1,0:T(8,128)(2,1)} %get-tuple-element.15.refs_0_, bf16[256,1024]{1,0:T(8,128)(2,1)} %get-tuple-element.16.refs_1_, ...), custom_call_target="tpu_custom_call" | custom-call | tf_op jit(solution)/shard_map/hand_over/pallas_call | solution.py:435

commit v4 on v3

--- a/solution.py
+++ b/solution.py
@@ -50,7 +50,7 @@
            doc, q_ref, k_ref, v_ref, og_ref, w_ref,
            ctx_out, dq_out, dk_out, dv_out, wg_out,
            wv, ogf, kc, pb, probs, ctxs, ogs, cga, cgt, own, dbuf, pair, back, acc,
-           s_w, s_up, s_dn, r_z, s_kv, r_kv, s_a, r_a, s_c, r_c, s_p, r_p, s_g, r_g):
+           s_w, s_up, s_dn, r_z, s_kv, r_kv, s_a, r_a, s_c, r_c, s_p, r_p, s_g, r_g, sums, s_s, r_s):
     me = lax.axis_index("seq")
     z = lax.axis_index("head")
     partner = flipped(me, 1)
@@ -97,10 +97,18 @@
     def kv_arrived(o):
         arrived(kc.at[:, pl.ds(starts[o], rows[o])], r_kv.at[o])
 
+    wide = seq_count // 2
+    my_half = lax.div(me, jnp.int32(wide))
+
+    def a_route(zp, j):
+        to = jnp.int32(zp * per_shard + j)
+        step = my_half - lax.div(to, jnp.int32(wide))
+        return to, to + step * wide, step * step
+
     def a_copy(zp, j):
-        to = zp * per_shard + j
-        return remote(ogf.at[zp, :, pl.ds(j * kcols, kcols)], ogs.at[me],
-                      s_a.at[to], r_a.at[me], seq=to)
+        to, dest, kind = a_route(zp, j)
+        return remote(ogf.at[zp, :, pl.ds(j * kcols, kcols)], ogs.at[kind, me],
+                      s_a.at[to], r_a.at[kind, me], seq=dest)
 
     def c_copy(o, n):
         part = pl.ds(n * (feats // 2), feats // 2)
@@ -117,6 +125,7 @@
                       s_g.at[g, o // 2], r_g.at[g, o // 2], seq=flipped(me, o))
 
     far = list(range(2, seq_count, 2))
+    near = [o for o in far if o < wide]
 
     for zp in range(head_count):
         w_copy(zp).start()
@@ -174,13 +183,15 @@
 
     def scatter_grad(zp):
         for j in range(per_shard):
-            @pl.when(zp * per_shard + j != me)
+            _, dest, kind = a_route(zp, j)
+
+            @pl.when(dest != me)
             def _():
                 a_copy(zp, j).start()
 
-            @pl.when(zp * per_shard + j == me)
+            @pl.when(dest == me)
             def _():
-                ogs[me] = ogf[zp, :, j * kcols:(j + 1) * kcols]
+                ogs[kind, me] = ogf[zp, :, j * kcols:(j + 1) * kcols]
 
     def project(zp, first=False):
         grad = ogf[zp]
@@ -212,16 +223,15 @@
 
         @pl.when(z >= k)
         def _():
-            if k > 1:
-                scatter_grad(z - k)
+            scatter_grad(z - k)
             project(z - k)
 
         @pl.when(z + k < head_count)
         def _():
-            if k > 1:
-                scatter_grad(z + k)
+            scatter_grad(z + k)
             project(z + k)
 
+    scatter_grad(z)
     for zp in range(head_count):
         w_copy(zp).wait()
     project(z, first=True)
@@ -233,15 +243,6 @@
     kv_arrived(1)
     for o in far:
         kv_arrived(o + 1)
-    scatter_grad(z)
-
-    @pl.when(z >= 1)
-    def _():
-        scatter_grad(z - 1)
-
-    @pl.when(z + 1 < head_count)
-    def _():
-        scatter_grad(z + 1)
 
     log2e = 1.4426950408889634
     my_doc = doc[0, me]
@@ -269,12 +270,12 @@
             ctx_out[:, at] = out.T.astype(BF16)
 
     forward(0, heads // 2)
-    for o in far + [1]:
+    for o in near + [1]:
         c_copy(o, 0).start()
     if head_count > 2:
         gather_step(2)
     forward(heads // 2, heads)
-    for o in far + [1]:
+    for o in near + [1]:
         c_copy(o, 1).start()
     for k in range(3, head_count):
         gather_step(k)
@@ -315,26 +316,32 @@
 
     finish(groups - 1)
 
-    for o in far:
+    for o in near:
         for n in range(2):
             c_copy(o, n).wait_recv()
             c_copy(o + 1, n).start()
-    for n, o in enumerate([0, 1] + far + [o + 1 for o in far]):
-        if o % 2 == 1:
-            for n in range(2):
-                c_copy(o, n).wait_recv()
-        src = flipped(me, o)
-        if o:
-            arrived(ogs.at[src], r_a.at[src])
-        grad = ogs[src]
-
-        @pl.loop(0, feats // 256)
-        def _(t):
-            at = pl.ds(pl.multiple_of(t * 256, 256), 256)
-            term = dot_nn(ctxs[o, at], grad)
-            acc[at] = term if n == 0 else acc[at] + term
-
-    wg_out[...] = acc[...].astype(BF16)
+
+    def share(kind, first):
+        for n, o in enumerate([0, 1] + near + [o + 1 for o in near]):
+            if o % 2 == 1 and first:
+                for part in range(2):
+                    c_copy(o, part).wait_recv()
+            src = flipped(me, o)
+            if o:
+                arrived(ogs.at[kind, src], r_a.at[kind, src])
+            grad = ogs[kind, src]
+
+            @pl.loop(0, feats // 256)
+            def _(t):
+                at = pl.ds(pl.multiple_of(t * 256, 256), 256)
+                term = dot_nn(ctxs[o, at], grad)
+                acc[at] = term if n == 0 else acc[at] + term
+
+    sum_copy = remote(sums.at[0], sums.at[1], s_s.at[0], r_s.at[0], seq=flipped(me, wide))
+    share(1, True)
+    sums[0] = acc[...].astype(BF16)
+    sum_copy.start()
+    share(0, False)
 
     far_rows = half - leaf
     r_id = lax.broadcasted_iota(jnp.int32, (leaf, far_rows), 0)
@@ -353,6 +360,9 @@
                 spread, back[g, which])
             out[:, g * gcols:(g + 1) * gcols] = total.astype(BF16)
 
+    sum_copy.wait()
+    wg_out[...] = (acc[...] + sums[1].astype(F32)).astype(BF16)
+
     for zp in range(head_count):
         @pl.when((z < head_count - 1) & (zp <= z))
         def _():
@@ -363,14 +373,14 @@
             down_copy(zp).wait_send()
 
         for j in range(per_shard):
-            @pl.when(zp * per_shard + j != me)
+            @pl.when(a_route(zp, j)[1] != me)
             def _():
                 a_copy(zp, j).wait_send()
     kv_copy(0).wait_send()
     for o in far:
         kv_copy(o).wait_send()
         kv_copy(o + 1).wait_send()
-    for o in range(1, seq_count):
+    for o in range(1, wide):
         for n in range(2):
             c_copy(o, n).wait_send()
     for g in range(groups):
@@ -410,8 +420,8 @@
             pltpu.VMEM((2, cols, feats), BF16),
             pltpu.VMEM((2, leaf, feats), BF16),
             pltpu.VMEM((heads, cols, leaf), BF16),
-            pltpu.VMEM((seq_count, feats, leaf), BF16),
-            pltpu.VMEM((seq_count, leaf, kcols), BF16),
+            pltpu.VMEM((seq_count // 2, feats, leaf), BF16),
+            pltpu.VMEM((2, seq_count, leaf, kcols), BF16),
             pltpu.VMEM((feats, leaf), F32),
             pltpu.VMEM((feats, leaf), BF16),
             pltpu.VMEM((groups, 2, leaf, gcols), F32),
@@ -420,9 +430,10 @@
             pltpu.VMEM((groups, 2, half - leaf, gcols), BF16),
             pltpu.VMEM((feats, kcols), F32),
             dma((head_count,)), dma((head_count,)), dma((head_count,)), dma((head_count,)),
-            dma((seq_count,)), dma((seq_count,)), dma((seq_count,)), dma((seq_count,)),
+            dma((seq_count,)), dma((seq_count,)), dma((seq_count,)), dma((2, seq_count)),
             dma((seq_count, 2)), dma((seq_count, 2)), dma((groups,)), dma((groups,)),
             dma((groups, seq_count // 2)), dma((groups, seq_count // 2)),
+            pltpu.VMEM((2, feats, kcols), BF16), dma((1,)), dma((1,)),
         ],
         compiler_params=pltpu.CompilerParams(
             collective_id=0, has_side_effects=True, vmem_limit_bytes=60 * 1024 * 1024),

time: 98.4 us -> 98.2 us (level)
  no operation moved by 1% of the time
where the time goes in v4:
time: 98.2 us; the launch traced here: 97.9 us
  Pallas kernels  97.3 us (99%)
    pallas_call x1, Pallas kernels, local(): pl.pallas_call(functools.partial(kernel, seq_count, head_count, leaf, fea...  93 us
    pallas_call x1, Pallas kernels, local(): pl.pallas_call(copy_kernel, grid=(steps,), out_shape=[jax.ShapeDtypeStruc...  4.25 us

profile of v4, /device:TPU:0, one launch (start us, length us, event | category | flops | bytes accessed | tf_op | source)
XLA Modules:
  0.0 97.9 jit_solution(7061924982735101398)
XLA Ops:
  0.6 93.0 %hier_attention.1 = (bf16[256,1024]{1,0:T(8,128)(2,1)}, bf16[256,1024]{1,0:T(8,128)(2,1)}, bf16[256,1024]{1,0:T(8,128)(2,1)}, bf16[256,1024]{1,0:T(8,128)(2,1)}, bf16[1024,512]{1,0:T(8,128)(2,1)}) custom-call(s32[1,8]{1,0:T(1,128)} %doc.1, bf16[256,1024]{1,0:T(8,128)(2,1)} %bitcast.8, bf16[256,1024]{1,0:T(8,128)(2,1)} %bitcast.9, ...), custom_call_target="tpu_custom_call" | custom-call | flops 8000000000 | bytes 16777216 | tf_op jit(solution)/shard_map/hier_attention/pallas_call | solution.py:411
  93.7 4.2 %hand_over.1 = (bf16[256,1024]{1,0:T(8,128)(2,1)}, bf16[256,1024]{1,0:T(8,128)(2,1)}, bf16[256,1024]{1,0:T(8,128)(2,1)}, bf16[256,1024]{1,0:T(8,128)(2,1)}, bf16[1024,512]{1,0:T(8,128)(2,1)}) custom-call(bf16[256,1024]{1,0:T(8,128)(2,1)} %get-tuple-element.15.refs_0_, bf16[256,1024]{1,0:T(8,128)(2,1)} %get-tuple-element.16.refs_1_, ...), custom_call_target="tpu_custom_call" | custom-call | tf_op jit(solution)/shard_map/hand_over/pallas_call | solution.py:446

commit v5 on v4

--- a/solution.py
+++ b/solution.py
@@ -290,8 +290,23 @@
         for o in far:
             g_copy(g, o).start()
 
-    @pl.loop(0, groups)
-    def _(g):
+    def share(kind, first):
+        for n, o in enumerate([0, 1] + near + [o + 1 for o in near]):
+            if o % 2 == 1 and first:
+                for part in range(2):
+                    c_copy(o, part).wait_recv()
+            src = flipped(me, o)
+            if o:
+                arrived(ogs.at[kind, src], r_a.at[kind, src])
+            grad = ogs[kind, src]
+
+            @pl.loop(0, feats // 256)
+            def _(t):
+                at = pl.ds(pl.multiple_of(t * 256, 256), 256)
+                term = dot_nn(ctxs[o, at], grad)
+                acc[at] = term if n == 0 else acc[at] + term
+
+    def backward(g):
         for i in range(GROUP_HEADS):
             h = g * GROUP_HEADS + i
             at = pl.ds(pl.multiple_of(h * DH, DH), DH)
@@ -314,33 +329,19 @@
         def _():
             finish(g - 1)
 
-    finish(groups - 1)
-
+    pl.loop(0, groups // 2)(backward)
     for o in near:
         for n in range(2):
             c_copy(o, n).wait_recv()
             c_copy(o + 1, n).start()
 
-    def share(kind, first):
-        for n, o in enumerate([0, 1] + near + [o + 1 for o in near]):
-            if o % 2 == 1 and first:
-                for part in range(2):
-                    c_copy(o, part).wait_recv()
-            src = flipped(me, o)
-            if o:
-                arrived(ogs.at[kind, src], r_a.at[kind, src])
-            grad = ogs[kind, src]
-
-            @pl.loop(0, feats // 256)
-            def _(t):
-                at = pl.ds(pl.multiple_of(t * 256, 256), 256)
-                term = dot_nn(ctxs[o, at], grad)
-                acc[at] = term if n == 0 else acc[at] + term
-
     sum_copy = remote(sums.at[0], sums.at[1], s_s.at[0], r_s.at[0], seq=flipped(me, wide))
     share(1, True)
     sums[0] = acc[...].astype(BF16)
     sum_copy.start()
+    pl.loop(groups // 2, groups)(backward)
+    finish(groups - 1)
+
     share(0, False)
 
     far_rows = half - leaf

time: 98.2 us -> 103 us (1.049)
  Pallas kernels: 97.3 us -> 102 us
    pallas_call x1, Pallas kernels: 93 us -> 97.5 us  [local(): pl.pallas_call(functools.partial(kernel, seq_count, head_count, leaf, fea...]
where the time goes in v5:
time: 103 us; the launch traced here: 102 us
  Pallas kernels  102 us (99%)
    pallas_call x1, Pallas kernels, local(): pl.pallas_call(functools.partial(kernel, seq_count, head_count, leaf, fea...  97.5 us
    pallas_call x1, Pallas kernels, local(): pl.pallas_call(copy_kernel, grid=(steps,), out_shape=[jax.ShapeDtypeStruc...  4.25 us

profile of v5, /device:TPU:0, one launch (start us, length us, event | category | flops | bytes accessed | tf_op | source)
XLA Modules:
  0.0 102.4 jit_solution(5517323338487395701)
XLA Ops:
  0.6 97.5 %hier_attention.1 = (bf16[256,1024]{1,0:T(8,128)(2,1)}, bf16[256,1024]{1,0:T(8,128)(2,1)}, bf16[256,1024]{1,0:T(8,128)(2,1)}, bf16[256,1024]{1,0:T(8,128)(2,1)}, bf16[1024,512]{1,0:T(8,128)(2,1)}) custom-call(s32[1,8]{1,0:T(1,128)} %doc.1, bf16[256,1024]{1,0:T(8,128)(2,1)} %bitcast.8, bf16[256,1024]{1,0:T(8,128)(2,1)} %bitcast.9, ...), custom_call_target="tpu_custom_call" | custom-call | flops 8000000000 | bytes 16777216 | tf_op jit(solution)/shard_map/hier_attention/pallas_call | solution.py:412
  98.1 4.2 %hand_over.1 = (bf16[256,1024]{1,0:T(8,128)(2,1)}, bf16[256,1024]{1,0:T(8,128)(2,1)}, bf16[256,1024]{1,0:T(8,128)(2,1)}, bf16[256,1024]{1,0:T(8,128)(2,1)}, bf16[1024,512]{1,0:T(8,128)(2,1)}) custom-call(bf16[256,1024]{1,0:T(8,128)(2,1)} %get-tuple-element.15.refs_0_, bf16[256,1024]{1,0:T(8,128)(2,1)} %get-tuple-element.16.refs_1_, ...), custom_call_target="tpu_custom_call" | custom-call | tf_op jit(solution)/shard_map/hand_over/pallas_call | solution.py:447
